TPU v7x, 128 devices: a whole 4x4x4 slice. The times are simulated.
128 devices in a mesh: hst: 16 (over z, x), doc: 8 (over y, core).
Axes of the slice: x: 4, y: 4, z: 4, core: 2. Of those that a mesh axis runs over, the one named last changes fastest.
Arguments:
- docs: bfloat16 [1048576, 768], P(('hst', 'doc')), may hold values from -400 to 400, as said below
- w_in: bfloat16 [768, 256], replicated, may hold values from -0.21875 to 0.21875
- w_out: bfloat16 [256, 64], replicated, may hold values from -0.375 to 0.375
- doc_host: int32 [1048576], P(('hst', 'doc')), may hold values from 0 to 2047
- tiles: bfloat16 [8192, 128, 128], P(('hst', 'doc')), may hold values from 0 to 10, as said below
- dst_block: int32 [8192], P(('hst', 'doc')), may hold values from 0 to 15
- src_block: int32 [8192], P(('hst', 'doc')), may hold values from 0 to 255
- tile_count: int32 [128], P(('hst', 'doc')), may hold values from 1 to 64, as said below
- teleport: int32 [32768], P('hst'), may hold values 0 or 1
Outputs:
- scores: float32 [32768, 64], P(('hst', 'doc'))
Inputs may be any that keep to these rules, and one draw needn't show every extreme that they name: `docs`: embeddings stay in the stated range. `tiles`: link weights are nonnegative. `tile_count`: some device uses all 64 slots.
All inputs are finite; a program needn't handle non-finite values. No bound on the sum of `teleport` on one device may be relied on, other than what follows from the above.
Results may differ from a plain program's by a relative error of at most 0.00066.
Values may be sent and summed in bfloat16 or wider, within the bound.
A program may use at most 128 MiB of HBM per device.

v0:
```python
import jax
import jax.numpy as jnp
from jax import lax
from jax.sharding import PartitionSpec as P

HOPS = 3


def body(docs, w_in, w_out, doc_host, tiles, dst_block, src_block, tile_count, teleport):
    host_dev = teleport.shape[0]
    block = tiles.shape[1]
    topics = w_out.shape[1]
    slots = tiles.shape[0]
    hosts_all = host_dev * lax.axis_size("hst")
    nblocks = hosts_all // block
    hidden = jax.nn.gelu(
        jnp.dot(docs, w_in, preferred_element_type=jnp.float32), approximate=True
    ).astype(jnp.bfloat16)
    probs = jax.nn.softmax(jnp.dot(hidden, w_out, preferred_element_type=jnp.float32), axis=-1)
    local_topic = jax.ops.segment_sum(probs, doc_host, num_segments=host_dev)
    used = (jnp.arange(slots) < tile_count[0]).astype(jnp.float32)
    colsum = jnp.sum(tiles, axis=1, dtype=jnp.float32)
    src_onehot = (src_block[:, None] == jnp.arange(nblocks)[None, :]).astype(jnp.float32) * used[
        :, None
    ]
    degree_blocks = jnp.dot(src_onehot.T, colsum, precision=lax.Precision.HIGHEST)
    degree = lax.psum(degree_blocks, ("hst", "doc")).reshape(hosts_all)
    own_degree = lax.dynamic_slice_in_dim(degree, lax.axis_index("hst") * host_dev, host_dev)
    inverse = 1.0 / jnp.maximum(own_degree, 1.0)
    dst_onehot = (dst_block[:, None] == jnp.arange(host_dev // block)[None, :]).astype(
        jnp.float32
    ) * used[:, None]
    member = teleport.astype(jnp.float32)
    rows = host_dev // lax.axis_size("doc")
    host_topic = lax.psum(local_topic, "doc")
    mass = lax.psum(jnp.sum(member[:, None] * host_topic, axis=0), "hst")
    tele = member[:, None] * host_topic / mass
    state = tele
    for hop in range(HOPS):
        sent = (state * inverse[:, None]).astype(jnp.bfloat16)
        full = lax.all_gather(sent, "hst", axis=0, tiled=True)
        slabs = full.reshape(nblocks, block, topics)[src_block]
        prod = jnp.einsum("kij,kjt->kit", tiles, slabs, preferred_element_type=jnp.float32)
        gathered = jnp.einsum("kb,kit->bit", dst_onehot, prod, precision=lax.Precision.HIGHEST)
        inflow = lax.psum(gathered.reshape(host_dev, topics), "doc")
        state = 0.85 * inflow + 0.15 * tele
    result = lax.dynamic_slice_in_dim(state, lax.axis_index("doc") * rows, rows)
    return hosts_all * result


def solution(mesh):
    placed = (
        P(("hst", "doc"), None),
        P(),
        P(),
        P(("hst", "doc")),
        P(("hst", "doc"), None, None),
        P(("hst", "doc")),
        P(("hst", "doc")),
        P(("hst", "doc")),
        P("hst"),
    )
    return jax.shard_map(
        body, mesh=mesh, in_specs=placed, out_specs=P(("hst", "doc"), None), check_vma=False
    )
```

profile of v0, /device:TPU:0, one launch (start us, length us, event | category | flops | bytes accessed | tf_op | source)
XLA Modules:
  0.0 640.4 jit_solution(17008999515403632906)
XLA Ops:
  7.3 2.1 convert_reduce_fusion
  11.2 8.6 %fusion.48 = (f32[8192]{0:T(1024)S(1)}, f32[8192,64]{0,1:T(8,128)S(1)}) fusion(bf16[256,64]{0,1:T(8,128)(2,1)} %param.11, bf16[8192,768]{1,0:T(8,128)(2,1)} %param.9, bf16[768,256]{1,0:T(8,128)(2,1)S(1)} %copy-done), kind=kOutput, calls=%fused_computation.78 | convolution fusion | flops 3509051392 | bytes 15138816 | tf_op jit(solution)/shard_map/dot_general | solution.py:19
  21.6 1.9 fusion.16
  23.5 2.7 copy.18
  26.2 44.5 %scatter_custom_fusion = f32[2048,64]{1,0:T(8,128)S(1)} fusion(s32[8192]{0:T(1024)} %param.12, f32[8192,64]{1,0:T(8,128)} %copy.18, f32[]{:T(128)} %constant.16.clone.1), kind=kCustom, calls=%fused_computation.37 | custom fusion | flops 524288 | bytes 524800 | tf_op jit(solution)/shard_map/scatter-add | solution.py:20
  72.0 82.8 %all-reduce.8.cloned.1.call-done = f32[32768]{0:T(1024)} async-done(((f32[32768]{0:T(1024)}), f32[32768]{0:T(1024)}) %all-reduce.8.cloned.1.call-update) | async-done | bytes 131088 | tf_op jit(solution)/shard_map/psum | solution.py:27
  155.5 59.7 %all-reduce.6.cloned.1.call-done = f32[2048,64]{0,1:T(8,128)} async-done(((f32[2048,64]{0,1:T(8,128)}), f32[2048,64]{0,1:T(8,128)}) %all-reduce.6.cloned.1.call-update) | async-done | bytes 524304 | tf_op jit(solution)/shard_map/psum | solution.py:35
  216.4 40.5 %psum.43 = f32[64]{0:T(128)S(1)} all-reduce(f32[64]{0:T(128)S(1)} %multiply_reduce_fusion), channel_id=1, replica_groups=mesh['hst'=16,'doc'=8] {'hst'}, use_global_device_ids=true, to_apply=%region_5.0 | all-reduce | flops 64 | bytes 512 | tf_op jit(solution)/shard_map/psum | solution.py:36
  259.7 44.7 %all-gather.4.cloned.1.call-done = bf16[32768,64]{0,1:T(8,128)(2,1)} async-done(((bf16[2048,64]{0,1:T(8,128)(2,1)}), bf16[32768,64]{0,1:T(8,128)(2,1)}) %all-gather.4.cloned.1.call-update) | async-done | bytes 4194320 | tf_op jit(solution)/shard_map/all_gather | solution.py:41
  304.4 5.4 copy_bitcast_fusion.2
  309.8 3.2 gather_fusion
  314.6 2.2 fusion.14
  317.8 60.4 %all-reduce.10.cloned.1.call-done = f32[2048,64]{0,1:T(8,128)} async-done(((f32[2048,64]{0,1:T(8,128)}), f32[2048,64]{0,1:T(8,128)}) %all-reduce.10.cloned.1.call-update) | async-done | bytes 524304 | tf_op jit(solution)/shard_map/psum | solution.py:45
  378.3 2.2 multiply_convert_fusion.1
  380.6 51.0 %all-gather.6.cloned.1.call-done = bf16[32768,64]{0,1:T(8,128)(2,1)} async-done(((bf16[2048,64]{0,1:T(8,128)(2,1)}), bf16[32768,64]{0,1:T(8,128)(2,1)}) %all-gather.6.cloned.1.call-update) | async-done | bytes 4194320 | tf_op jit(solution)/shard_map/all_gather | solution.py:41
  431.6 5.4 copy_bitcast_fusion.1
  436.9 3.1 gather_fusion.1
  441.6 2.2 fusion.12
  444.8 60.4 %all-reduce.12.cloned.1.call-done = f32[2048,64]{0,1:T(8,128)} async-done(((f32[2048,64]{0,1:T(8,128)}), f32[2048,64]{0,1:T(8,128)}) %all-reduce.12.cloned.1.call-update) | async-done | bytes 524304 | tf_op jit(solution)/shard_map/psum | solution.py:45
  507.4 51.0 %all-gather.8.cloned.1.call-done = bf16[32768,64]{0,1:T(8,128)(2,1)} async-done(((bf16[2048,64]{0,1:T(8,128)(2,1)}), bf16[32768,64]{0,1:T(8,128)(2,1)}) %all-gather.8.cloned.1.call-update) | async-done | bytes 4194320 | tf_op jit(solution)/shard_map/all_gather | solution.py:41
  558.4 5.4 copy_bitcast_fusion
  563.7 3.1 gather_fusion.2
  568.3 2.2 fusion.10
  571.6 60.5 %all-reduce.14.cloned.1.call-done = f32[2048,64]{0,1:T(8,128)} async-done(((f32[2048,64]{0,1:T(8,128)}), f32[2048,64]{0,1:T(8,128)}) %all-reduce.14.cloned.1.call-update) | async-done | bytes 524304 | tf_op jit(solution)/shard_map/psum | solution.py:45
  (62 shorter events, 20.6 us)
Async XLA Ops:
  6.5 4.7 copy-start
  6.5 148.3 %all-reduce.8.cloned.1.call-start = ((), (), s32[]{:S(2)}) async-start(), calls=%async_computation.1 | async-start | bytes 262144 | tf_op jit(solution)/shard_map/psum | solution.py:27
  7.3 2.1 copy-start.5
  11.2 204.0 %all-reduce.6.cloned.1.call-start = ((), (), s32[]{:S(2)}) async-start(), calls=%async_computation | async-start | bytes 1048576 | tf_op jit(solution)/shard_map/psum | solution.py:35
  19.9 1.3 copy-start.2
  23.5 48.5 %copy-start.8 = (s32[2048]{0:T(1024)S(1)}, s32[2048]{0:T(1024)}, u32[]{:S(2)}) copy-start(s32[2048]{0:T(1024)} %param.17) | copy-start | bytes 24580
  23.5 235.5 %copy-start.13 = (s32[64]{0:T(128)S(1)}, s32[64]{0:T(128)}, u32[]{:S(2)}) copy-start(s32[64]{0:T(128)} %param.15) | copy-start | bytes 772
  71.9 232.4 %all-gather.4.cloned.1.call-start = ((), (), s32[]{:S(2)}) async-start(), calls=%async_computation.2 | async-start | bytes 4456448 | tf_op jit(solution)/shard_map/all_gather | solution.py:41
  256.9 47.5 %copy-start.11 = (f32[64]{0:T(128)}, f32[64]{0:T(128)S(1)}, u32[]{:S(2)}) copy-start(f32[64]{0:T(128)S(1)} %psum.43) | copy-start | bytes 772
  258.8 119.5 %all-reduce.10.cloned.1.call-start = ((), (), s32[]{:S(2)}) async-start(), calls=%async_computation.3 | async-start | bytes 1048576 | tf_op jit(solution)/shard_map/psum | solution.py:45
  309.8 3.2 copy-start.1
  313.0 1.6 copy-start.6
  313.0 1.6 copy-start.9
  314.6 63.7 %copy-start.3 = (f32[2048,64]{0,1:T(8,128)S(1)}, f32[2048,64]{0,1:T(8,128)}, u32[]{:S(2)}) copy-start(f32[2048,64]{0,1:T(8,128)} %all-reduce.6.cloned.1.call-done) | copy-start | bytes 1572868
  314.6 63.7 %copy-start.12 = (f32[64]{0:T(128)S(1)}, f32[64]{0:T(128)}, u32[]{:S(2)}) copy-start(f32[64]{0:T(128)} %copy-done.11) | copy-start | bytes 772
  317.8 113.8 %all-gather.6.cloned.1.call-start = ((), (), s32[]{:S(2)}) async-start(), calls=%async_computation.4 | async-start | bytes 4456448 | tf_op jit(solution)/shard_map/all_gather | solution.py:41
  380.5 124.8 %all-reduce.12.cloned.1.call-start = ((), (), s32[]{:S(2)}) async-start(), calls=%async_computation.5 | async-start | bytes 1048576 | tf_op jit(solution)/shard_map/psum | solution.py:45
  436.9 4.6 copy-start.7
  436.9 4.6 copy-start.10
  441.6 63.7 %copy-start.4 = (f32[2048,64]{0,1:T(8,128)S(1)}, f32[2048,64]{0,1:T(8,128)}, u32[]{:S(2)}) copy-start(f32[2048,64]{0,1:T(8,128)} %get-tuple-element.6) | copy-start | bytes 1572868
  444.8 113.6 %all-gather.8.cloned.1.call-start = ((), (), s32[]{:S(2)}) async-start(), calls=%async_computation.6 | async-start | bytes 4456448 | tf_op jit(solution)/shard_map/all_gather | solution.py:41
  507.1 124.9 %all-reduce.14.cloned.1.call-start = ((), (), s32[]{:S(2)}) async-start(), calls=%async_computation.7 | async-start | bytes 1048576 | tf_op jit(solution)/shard_map/psum | solution.py:45
Sparse Core Ops, SparseCore 0:
  12.1 142.6 all-reduce.7
  157.2 57.9 all-reduce.5
  258.9 45.3 all-gather.3
  317.9 60.3 all-reduce.9
  380.6 50.8 all-gather.5
  444.9 60.3 all-reduce.11
  507.4 50.8 all-gather.7
  571.7 60.3 all-reduce.13
where the time goes:
time: 641 us; the launch traced here: 640 us
  waiting for transfers between devices  471 us (73%)
  other arithmetic  58.8 us (9%)
  blocking collectives  40.5 us (6%)
  local copies, waits for them, and re-layouts  33.6 us (5%)
  matrix products  21.7 us (3%)
  between operations  14.4 us (2%)
    psum x3, waiting for transfers between devices, body(): inflow = lax.psum(gathered.reshape(host_dev, topics), 'doc')  181 us
    all_gather x3, waiting for transfers between devices, body(): full = lax.all_gather(sent, 'hst', axis=0, tiled=True)  147 us
    psum x1, waiting for transfers between devices, body(): degree = lax.psum(degree_blocks, ('hst', 'doc')).reshape(hosts_all)  82.8 us
    psum x1, waiting for transfers between devices, body(): host_topic = lax.psum(local_topic, 'doc')  59.7 us
    scatter-add x1, other arithmetic, body(): local_topic = jax.ops.segment_sum(probs, doc_host, num_segments=host_dev)  44.5 us
    psum x1, blocking collectives, body(): mass = lax.psum(jnp.sum(member[:, None] * host_topic, axis=0), 'hst')  40.5 us
    reshape x3, local copies, waits for them, and re-layouts, body(): slabs = full.reshape(nblocks, block, topics)[src_block]  16.1 us
  transfers between devices with their start and end apart: 8, of which 8 were waited for; matrix products, arithmetic and copies ran while one was open for 9% of the time, Pallas kernels for 0%

commit v1 on v0

--- a/solution.py
+++ b/solution.py
@@ -24,7 +24,7 @@
         :, None
     ]
     degree_blocks = jnp.dot(src_onehot.T, colsum, precision=lax.Precision.HIGHEST)
-    degree = lax.psum(degree_blocks, ("hst", "doc")).reshape(hosts_all)
+    degree = lax.psum(lax.psum(degree_blocks, "doc"), "hst").reshape(hosts_all)
     own_degree = lax.dynamic_slice_in_dim(degree, lax.axis_index("hst") * host_dev, host_dev)
     inverse = 1.0 / jnp.maximum(own_degree, 1.0)
     dst_onehot = (dst_block[:, None] == jnp.arange(host_dev // block)[None, :]).astype(

time: 641 us -> 609 us (0.950)
  waiting for transfers between devices: 471 us -> 441 us
    psum x1, waiting for transfers between devices: 82.8 us -> 43 us  [body(): degree = lax.psum(lax.psum(degree_blocks, 'doc'), 'hst').reshape(hosts_all)]
  transfers between devices with their start and end apart: 8 -> 8, of which waited for: 8 -> 8; matrix products, arithmetic and copies ran while one was open for 9% -> 0% of each run, Pallas kernels for 0% -> 0%
where the time goes in v1:
time: 609 us
  waiting for transfers between devices  441 us (72%)
  other arithmetic  57.5 us (9%)
  blocking collectives  40.5 us (7%)
  local copies, waits for them, and re-layouts  34.3 us (6%)
  matrix products  21 us (3%)
  between operations  14.4 us (2%)
    psum x3, waiting for transfers between devices, body(): inflow = lax.psum(gathered.reshape(host_dev, topics), 'doc')  181 us
    all_gather x3, waiting for transfers between devices, body(): full = lax.all_gather(sent, 'hst', axis=0, tiled=True)  152 us
    psum x1, waiting for transfers between devices, body(): host_topic = lax.psum(local_topic, 'doc')  63.9 us
    scatter-add x1, other arithmetic, body(): local_topic = jax.ops.segment_sum(probs, doc_host, num_segments=host_dev)  44.5 us
    psum x1, waiting for transfers between devices, body(): degree = lax.psum(lax.psum(degree_blocks, 'doc'), 'hst').reshape(hosts_all)  43 us
    psum x1, blocking collectives, body(): mass = lax.psum(jnp.sum(member[:, None] * host_topic, axis=0), 'hst')  40.5 us
    reshape x3, local copies, waits for them, and re-layouts, body(): slabs = full.reshape(nblocks, block, topics)[src_block]  16.1 us
  transfers between devices with their start and end apart: 8, of which 8 were waited for; matrix products, arithmetic and copies ran while one was open for 0% of the time, Pallas kernels for 0%

profile of v1, /device:TPU:0, one launch (start us, length us, event | category | flops | bytes accessed | tf_op | source)
XLA Modules:
  0.0 608.8 jit_solution(18392386837641658097)
XLA Ops:
  7.5 8.6 %fusion.49 = (f32[8192]{0:T(1024)S(1)}, f32[8192,64]{0,1:T(8,128)S(1)}) fusion(bf16[256,64]{0,1:T(8,128)(2,1)} %param.11, bf16[8192,768]{1,0:T(8,128)(2,1)} %param.9, bf16[768,256]{1,0:T(8,128)(2,1)S(1)} %copy-done), kind=kOutput, calls=%fused_computation.78 | convolution fusion | flops 3509051392 | bytes 15138816 | tf_op jit(solution)/shard_map/dot_general | solution.py:19
  18.2 3.9 copy.18
  22.1 44.5 %scatter_custom_fusion = f32[2048,64]{1,0:T(8,128)S(1)} fusion(s32[8192]{0:T(1024)} %param.12, f32[8192,64]{1,0:T(8,128)} %copy.18, f32[]{:T(128)} %constant.16.clone.1), kind=kCustom, calls=%fused_computation.36 | custom fusion | flops 524288 | bytes 524800 | tf_op jit(solution)/shard_map/scatter-add | solution.py:20
  70.2 63.9 %all-reduce.15.cloned.1.call-done = (f32[2048,64]{0,1:T(8,128)}, f32[256,128]{1,0:T(8,128)}) async-done(((f32[2048,64]{0,1:T(8,128)}, f32[256,128]{1,0:T(8,128)}), (f32[2048,64]{0,1:T(8,128)}, f32[256,128]{1,0:T(8,128)})) %all-reduce.15.cloned.1.call-update) | async-done | bytes 655376 | tf_op jit(solution)/shard_map/psum | solution.py:35
  135.4 40.5 %psum.50 = f32[64]{0:T(128)S(1)} all-reduce(f32[64]{0:T(128)S(1)} %multiply_reduce_fusion), channel_id=1, replica_groups=mesh['hst'=16,'doc'=8] {'hst'}, use_global_device_ids=true, to_apply=%region_5.0 | all-reduce | flops 64 | bytes 512 | tf_op jit(solution)/shard_map/psum | solution.py:36
  175.9 43.0 %all-reduce.7.cloned.1.call-done = f32[32768]{0:T(1024)} async-done(((f32[32768]{0:T(1024)}), f32[32768]{0:T(1024)}) %all-reduce.7.cloned.1.call-update) | async-done | bytes 131088 | tf_op jit(solution)/shard_map/psum | solution.py:27
  219.6 1.9 multiply_convert_fusion.2
  222.9 49.8 %all-gather.4.cloned.1.call-done = bf16[32768,64]{0,1:T(8,128)(2,1)} async-done(((bf16[2048,64]{0,1:T(8,128)(2,1)}), bf16[32768,64]{0,1:T(8,128)(2,1)}) %all-gather.4.cloned.1.call-update) | async-done | bytes 4194320 | tf_op jit(solution)/shard_map/all_gather | solution.py:41
  272.7 5.4 copy_bitcast_fusion.2
  278.1 3.1 gather_fusion
  282.7 2.2 fusion.14
  286.2 60.2 %all-reduce.9.cloned.1.call-done = f32[2048,64]{0,1:T(8,128)} async-done(((f32[2048,64]{0,1:T(8,128)}), f32[2048,64]{0,1:T(8,128)}) %all-reduce.9.cloned.1.call-update) | async-done | bytes 524304 | tf_op jit(solution)/shard_map/psum | solution.py:45
  346.4 2.2 multiply_convert_fusion.1
  348.7 51.0 %all-gather.6.cloned.1.call-done = bf16[32768,64]{0,1:T(8,128)(2,1)} async-done(((bf16[2048,64]{0,1:T(8,128)(2,1)}), bf16[32768,64]{0,1:T(8,128)(2,1)}) %all-gather.6.cloned.1.call-update) | async-done | bytes 4194320 | tf_op jit(solution)/shard_map/all_gather | solution.py:41
  399.7 5.4 copy_bitcast_fusion.1
  405.1 3.1 gather_fusion.1
  409.7 2.2 fusion.12
  413.0 60.5 %all-reduce.11.cloned.1.call-done = f32[2048,64]{0,1:T(8,128)} async-done(((f32[2048,64]{0,1:T(8,128)}), f32[2048,64]{0,1:T(8,128)}) %all-reduce.11.cloned.1.call-update) | async-done | bytes 524304 | tf_op jit(solution)/shard_map/psum | solution.py:45
  473.4 1.8 multiply_convert_fusion
  475.3 51.4 %all-gather.8.cloned.1.call-done = bf16[32768,64]{0,1:T(8,128)(2,1)} async-done(((bf16[2048,64]{0,1:T(8,128)(2,1)}), bf16[32768,64]{0,1:T(8,128)(2,1)}) %all-gather.8.cloned.1.call-update) | async-done | bytes 4194320 | tf_op jit(solution)/shard_map/all_gather | solution.py:41
  526.7 5.4 copy_bitcast_fusion
  532.1 3.1 gather_fusion.2
  536.7 2.2 fusion.10
  539.9 60.5 %all-reduce.13.cloned.1.call-done = f32[2048,64]{0,1:T(8,128)} async-done(((f32[2048,64]{0,1:T(8,128)}), f32[2048,64]{0,1:T(8,128)}) %all-reduce.13.cloned.1.call-update) | async-done | bytes 524304 | tf_op jit(solution)/shard_map/psum | solution.py:45
  (60 shorter events, 18.5 us)
Async XLA Ops:
  6.5 1.0 copy-start
  6.5 127.6 %all-reduce.15.cloned.1.call-start = ((), (), s32[]{:S(2)}) async-start(), calls=%async_computation.7 | async-start | bytes 1310720 | tf_op jit(solution)/shard_map/psum | solution.py:35
  18.1 50.3 %copy-start.1 = (bf16[64,128,128]{2,1,0:T(8,128)(2,1)S(1)}, bf16[64,128,128]{2,1,0:T(8,128)(2,1)}, u32[]{:S(2)}) copy-start(bf16[64,128,128]{2,1,0:T(8,128)(2,1)} %param.13) | copy-start | bytes 6291460
  18.2 50.8 %copy-start.12 = (s32[64]{0:T(128)S(1)}, s32[64]{0:T(128)}, u32[]{:S(2)}) copy-start(s32[64]{0:T(128)} %param.15) | copy-start | bytes 772
  22.1 48.1 %copy-start.7 = (s32[2048]{0:T(1024)S(1)}, s32[2048]{0:T(1024)}, u32[]{:S(2)}) copy-start(s32[2048]{0:T(1024)} %param.17) | copy-start | bytes 24580
  68.4 0.5 copy-start.4
  70.1 148.8 %all-reduce.7.cloned.1.call-start = ((), (), s32[]{:S(2)}) async-start(), calls=%async_computation | async-start | bytes 262144 | tf_op jit(solution)/shard_map/psum | solution.py:27
  134.2 138.5 %all-gather.4.cloned.1.call-start = ((), (), s32[]{:S(2)}) async-start(), calls=%async_computation.1 | async-start | bytes 4456448 | tf_op jit(solution)/shard_map/all_gather | solution.py:41
  175.9 96.8 %copy-start.10 = (f32[64]{0:T(128)}, f32[64]{0:T(128)S(1)}, u32[]{:S(2)}) copy-start(f32[64]{0:T(128)S(1)} %psum.50) | copy-start | bytes 772
  221.5 124.9 %all-reduce.9.cloned.1.call-start = ((), (), s32[]{:S(2)}) async-start(), calls=%async_computation.2 | async-start | bytes 1048576 | tf_op jit(solution)/shard_map/psum | solution.py:45
  281.1 1.6 copy-start.5
  281.2 1.6 copy-start.8
  282.7 63.7 %copy-start.2 = (f32[2048,64]{0,1:T(8,128)S(1)}, f32[2048,64]{0,1:T(8,128)}, u32[]{:S(2)}) copy-start(f32[2048,64]{0,1:T(8,128)} %get-tuple-element.5) | copy-start | bytes 1572868
  282.7 63.7 %copy-start.11 = (f32[64]{0:T(128)S(1)}, f32[64]{0:T(128)}, u32[]{:S(2)}) copy-start(f32[64]{0:T(128)} %copy-done.10) | copy-start | bytes 772
  286.0 113.7 %all-gather.6.cloned.1.call-start = ((), (), s32[]{:S(2)}) async-start(), calls=%async_computation.3 | async-start | bytes 4456448 | tf_op jit(solution)/shard_map/all_gather | solution.py:41
  348.6 124.8 %all-reduce.11.cloned.1.call-start = ((), (), s32[]{:S(2)}) async-start(), calls=%async_computation.4 | async-start | bytes 1048576 | tf_op jit(solution)/shard_map/psum | solution.py:45
  405.1 4.6 copy-start.6
  405.1 4.6 copy-start.9
  409.7 63.8 %copy-start.3 = (f32[2048,64]{0,1:T(8,128)S(1)}, f32[2048,64]{0,1:T(8,128)}, u32[]{:S(2)}) copy-start(f32[2048,64]{0,1:T(8,128)} %get-tuple-element.8) | copy-start | bytes 1572868
  412.9 113.8 %all-gather.8.cloned.1.call-start = ((), (), s32[]{:S(2)}) async-start(), calls=%async_computation.5 | async-start | bytes 4456448 | tf_op jit(solution)/shard_map/all_gather | solution.py:41
  475.3 125.1 %all-reduce.13.cloned.1.call-start = ((), (), s32[]{:S(2)}) async-start(), calls=%async_computation.6 | async-start | bytes 1048576 | tf_op jit(solution)/shard_map/psum | solution.py:45
Sparse Core Ops, SparseCore 0:
  70.2 63.8 all-reduce.14
  137.3 81.5 all-reduce.6
  221.7 50.9 all-gather.3
  286.1 60.3 all-reduce.8
  348.8 50.8 all-gather.5
  413.0 60.3 all-reduce.10
  475.8 50.8 all-gather.7
  540.1 60.3 all-reduce.12
